TPU v7x, 32 devices: a whole 2x2x4 slice. The times are simulated.
32 devices in a mesh: lat: 4 (over z), lon: 4 (over y, core), buf: 2 (over x).
Axes of the slice: x: 2, y: 2, z: 4, core: 2. Of those that a mesh axis runs over, the one named last changes fastest.
Arguments:
- store: bfloat16 [8, 64, 64, 1725], P('buf', ('lat', 'lon')), may hold values from -6 to 6
- sample_index: int32 [6], replicated, may hold values from 0 to 7, as said below
- region_ids: int32 [64, 64], replicated, may hold values from 0 to 2
- w_embed: bfloat16 [1725, 512], replicated, may hold values from -0.15625 to 0.15625
- attn_gain: float32 [512], replicated, may hold values from 0.1 to 1.9
- w_qkv: bfloat16 [512, 1536], replicated, may hold values from -8 to 8
- w_out: bfloat16 [512, 512], replicated, may hold values from -0.25 to 0.25
- out_gain: float32 [512], replicated, may hold values from 0.1 to 1.9
- w_dec: bfloat16 [512, 1725], replicated, may hold values from -0.25 to 0.25
Outputs:
- new_store: bfloat16 [8, 64, 64, 1725], P('buf', ('lat', 'lon'))
Inputs may be any that keep to these rules, and one draw needn't show every extreme that they name: `sample_index`: distinct slot numbers.
All inputs are finite; a program needn't handle non-finite values.
Results may differ from a plain program's by a relative error of at most 0.007.
Values may be sent and summed in bfloat16 or wider, within the bound.
A program may use at most 128 MiB of HBM per device.

v0:
```python
import math

import jax
import jax.numpy as jnp
from jax import lax
from jax.sharding import PartitionSpec as P

D = 512
HEADS = 8
HDIM = 64
WIN = 8


def with_halo(array, sides, width):
    for axis, dim in sides:
        devices, length = (lax.axis_size(axis), array.shape[dim])
        up = [(i, (i + 1) % devices) for i in range(devices)]
        down = [(j, i) for i, j in up]
        last = lax.slice_in_dim(array, length - width, length, axis=dim)
        leading = lax.slice_in_dim(array, 0, width, axis=dim)
        before = lax.ppermute(last, axis, up)
        after = lax.ppermute(leading, axis, down)
        array = jnp.concatenate([before, array, after], axis=dim)
    return array


def layer_norm(values, gain_row):
    center = jnp.mean(values, axis=-1, keepdims=True)
    spread = jnp.mean(jnp.square(values - center), axis=-1, keepdims=True)
    return (values - center) * lax.rsqrt(spread + 1e-05) * gain_row


def window_mix(windows, regions):
    scores = jnp.einsum(
        "bwqhd,bwkhd->bwhqk",
        windows[:, :, :, 0],
        windows[:, :, :, 1],
        preferred_element_type=jnp.float32,
    ) / math.sqrt(HDIM)
    visible = (regions[:, :, None] == regions[:, None, :])[None, :, None]
    scores = jnp.where(visible, scores, -1e30)
    highest = jnp.max(scores, axis=-1, keepdims=True)
    expo_terms = jnp.where(visible, jnp.exp(scores - highest), 0.0)
    weights = (expo_terms / jnp.sum(expo_terms, axis=-1, keepdims=True)).astype(jnp.bfloat16)
    return jnp.einsum(
        "bwhqk,bwkhd->bwqhd", weights, windows[:, :, :, 2], preferred_element_type=jnp.float32
    ).astype(jnp.bfloat16)


def local(store, sample_index, region_ids, w_embed, attn_gain, w_qkv, w_out, out_gain, w_dec):
    lon_count = lax.axis_size("lon")
    slots_here, rows_here, width_all, patch_len = store.shape
    patch_cols = width_all // lon_count
    patch_rows = rows_here * lon_count
    half_win = WIN // 2
    ext_rows = patch_rows + WIN
    ext_cols = patch_cols + WIN
    own_slots = lax.axis_index("buf") * slots_here + jnp.arange(slots_here, dtype=jnp.int32)
    matches = own_slots[:, None] == sample_index[None, :]
    occupied = jnp.any(matches, axis=1)
    local_rows = store.reshape(slots_here, 1, rows_here, lon_count, patch_cols, patch_len)
    tile_data = lax.all_to_all(local_rows, "lon", split_axis=3, concat_axis=1, tiled=True)
    patches = tile_data.reshape(-1, patch_len)
    embedded = jnp.dot(patches, w_embed, preferred_element_type=jnp.float32).astype(jnp.bfloat16)
    normed = layer_norm(embedded.astype(jnp.float32), attn_gain).astype(jnp.bfloat16)
    normed = normed.reshape(slots_here, patch_rows, patch_cols, D)
    widened = with_halo(normed, (("lat", 1), ("lon", 2)), half_win)
    projected = jnp.dot(widened.reshape(-1, D), w_qkv, preferred_element_type=jnp.float32).astype(
        jnp.bfloat16
    )
    windows = projected.reshape(
        slots_here, ext_rows // WIN, WIN, ext_cols // WIN, WIN, 3, HEADS, HDIM
    )
    windows = windows.transpose(0, 1, 3, 2, 4, 5, 6, 7).reshape(
        slots_here, -1, WIN * WIN, 3, HEADS, HDIM
    )
    total_rows, total_cols = region_ids.shape
    row_pick = (
        lax.axis_index("lat") * patch_rows - half_win + jnp.arange(ext_rows, dtype=jnp.int32)
    ) % total_rows
    col_pick = (
        lax.axis_index("lon") * patch_cols - half_win + jnp.arange(ext_cols, dtype=jnp.int32)
    ) % total_cols
    local_regions = jnp.take(jnp.take(region_ids, row_pick, axis=0), col_pick, axis=1)
    region_windows = (
        local_regions.reshape(ext_rows // WIN, WIN, ext_cols // WIN, WIN)
        .transpose(0, 2, 1, 3)
        .reshape(-1, WIN * WIN)
    )
    mixed_heads = window_mix(windows, region_windows)
    placed = mixed_heads.reshape(slots_here, ext_rows // WIN, ext_cols // WIN, WIN, WIN, D)
    placed = placed.transpose(0, 1, 3, 2, 4, 5).reshape(slots_here, ext_rows, ext_cols, D)
    placed = placed[:, half_win : half_win + patch_rows, half_win : half_win + patch_cols].reshape(
        -1, D
    )
    updated = embedded.astype(jnp.float32) + jnp.dot(
        placed, w_out, preferred_element_type=jnp.float32
    )
    final_norm = layer_norm(updated, out_gain).astype(jnp.bfloat16)
    predicted = (
        patches.astype(jnp.float32) + jnp.dot(final_norm, w_dec, preferred_element_type=jnp.float32)
    ).astype(jnp.bfloat16)
    outgoing = predicted.reshape(slots_here, lon_count, rows_here, 1, patch_cols, patch_len)
    returned = lax.all_to_all(outgoing, "lon", split_axis=1, concat_axis=3, tiled=True)
    strip_data = returned.reshape(slots_here, rows_here, width_all, patch_len)
    return jnp.where(occupied[:, None, None, None], strip_data, store)


def solution(mesh):
    return jax.shard_map(
        local,
        mesh=mesh,
        in_specs=(P("buf", ("lat", "lon"), None, None), P(), P(), P(), P(), P(), P(), P(), P()),
        out_specs=P("buf", ("lat", "lon"), None, None),
        check_vma=False,
    )
```

profile of v0, /device:TPU:1, one launch (start us, length us, event | category | flops | bytes accessed | tf_op | source)
XLA Modules:
  0.0 231.1 jit_solution(15052900297631613152)
XLA Ops:
  0.0 0.0 copy-start
  0.0 4.4 %copy.71 = bf16[4,1,4,4,16,1725]{5,4,2,0,1,3:T(8,128)(2,1)} copy(bf16[4,1,4,4,16,1725]{5,4,3,2,0,1:T(8,128)(2,1)} %bitcast.55) | data formatting | bytes 7065600 | tf_op jit(solution)/shard_map/reshape | solution.py:61
  4.4 4.9 %all-to-all-start = ((bf16[4,1,4,4,16,1725]{5,4,2,0,1,3:T(8,128)(2,1)}), bf16[4,1,4,4,16,1725]{5,4,2,0,1,3:T(8,128)(2,1)}, u32[]{:S(2)}, u32[]{:S(2)}) async-start(bf16[4,1,4,4,16,1725]{5,4,2,0,1,3:T(8,128)(2,1)} %copy.71), calls=%async_computation | async-start | bytes 7340032 | tf_op jit(solution)/shard_map/all_to_all | solution.py:62
  9.4 0.0 copy-done.7
  9.4 0.6 gather_fusion
  10.0 0.1 broadcast_select_fusion.1
  10.0 41.3 %all-to-all-done = bf16[4,1,4,4,16,1725]{5,4,2,0,1,3:T(8,128)(2,1)} async-done(((bf16[4,1,4,4,16,1725]{5,4,2,0,1,3:T(8,128)(2,1)}), bf16[4,1,4,4,16,1725]{5,4,2,0,1,3:T(8,128)(2,1)}, u32[]{:S(2)}, u32[]{:S(2)}) %all-to-all-start) | async-done | bytes 3532832 | tf_op jit(solution)/shard_map/all_to_all | solution.py:62
  51.4 2.4 %copy.72 = bf16[4,4,1,4,1,16,1725]{6,5,3,1,0,4,2:T(8,128)(2,1)S(1)} copy(bf16[4,4,1,4,1,16,1725]{6,5,3,0,1,4,2:T(8,128)(2,1)} %bitcast.2) | data formatting | bytes 7065600 | tf_op jit(solution)/shard_map/all_to_all | solution.py:62
  53.8 0.0 copy-start.1
  53.8 0.2 copy-done.9
  53.9 2.1 convert_reduce_fusion
  56.1 0.0 copy-done.1
  56.1 0.0 copy-start.3
  56.1 0.5 fusion.10
  56.6 0.4 copy-done.3
  57.1 0.0 copy-done.8
  57.1 0.4 fusion.12
  57.5 0.8 fusion.24
  58.3 2.5 %collective-permute-start = (bf16[4,4,16,512]{3,2,1,0:T(8,128)(2,1)}, bf16[4,4,16,512]{3,2,1,0:T(8,128)(2,1)S(1)}, u32[]{:S(2)}, u32[]{:S(2)}) collective-permute-start(bf16[4,4,16,512]{3,2,1,0:T(8,128)(2,1)} %get-tuple-element.7), channel_id=1, source_target_pairs={{0,8},{8,16},{16,24},{24,0},{1,9},{9,17},{17,25},{25,1},{2,10},{10... | collective-permute-start | bytes 786440 | tf_op jit(solution)/shard_map/ppermute | solution.py:21
  60.8 2.0 collective-permute-start.1
  62.9 0.1 copy.75
  63.0 0.6 gather_fusion.1
  63.5 0.1 copy.76
  63.6 0.1 gather.12
  63.7 5.2 %collective-permute-done = bf16[4,4,16,512]{3,2,1,0:T(8,128)(2,1)S(1)} collective-permute-done((bf16[4,4,16,512]{3,2,1,0:T(8,128)(2,1)}, bf16[4,4,16,512]{3,2,1,0:T(8,128)(2,1)S(1)}, u32[]{:S(2)}, u32[]{:S(2)}) %collective-permute-start) | collective-permute-done | bytes 262176 | tf_op jit(solution)/shard_map/ppermute | solution.py:21
  68.9 5.3 %collective-permute-done.1 = bf16[4,4,16,512]{3,2,1,0:T(8,128)(2,1)S(1)} collective-permute-done((bf16[4,4,16,512]{3,2,1,0:T(8,128)(2,1)}, bf16[4,4,16,512]{3,2,1,0:T(8,128)(2,1)S(1)}, u32[]{:S(2)}, u32[]{:S(2)}) %collective-permute-start.1) | collective-permute-done | bytes 262176 | tf_op jit(solution)/shard_map/ppermute | solution.py:22
  74.3 1.2 pad_maximum_fusion.3
  75.5 1.4 collective-permute-start.2
  76.8 0.0 collective-permute-start.3
  76.9 0.1 eq.38
  76.9 0.2 broadcast_compare_fusion
  77.1 5.9 %copy.73 = bf16[1024,1725]{0,1:T(8,128)(2,1)} copy(bf16[1024,1725]{1,0:T(8,128)(2,1)} %bitcast.53) | data formatting | bytes 7065600 | tf_op jit(solution)/shard_map/reshape | solution.py:63
  83.0 1.3 collective-permute-done.2
  84.3 3.3 %collective-permute-done.3 = bf16[4,24,4,512]{3,2,1,0:T(4,128)(2,1)} collective-permute-done((bf16[4,24,4,512]{3,2,1,0:T(4,128)(2,1)}, bf16[4,24,4,512]{3,2,1,0:T(4,128)(2,1)}, u32[]{:S(2)}, u32[]{:S(2)}) %collective-permute-start.3) | collective-permute-done | bytes 393248 | tf_op jit(solution)/shard_map/ppermute | solution.py:22
  87.6 2.8 %pad_maximum_fusion = bf16[4,24,24,512]{3,2,1,0:T(8,128)(2,1)S(1)} fusion(bf16[4,24,4,512]{3,2,1,0:T(4,128)(2,1)} %collective-permute-done.3, bf16[4,4,16,512]{3,2,1,0:T(8,128)(2,1)S(1)} %collective-permute-done.1, bf16[4,16,16,512]{3,2,1,0:T(8,128)(2,1)S(1)} %bitcast.59, bf16[4,4,16,512]{3,2,1,0:T(8,128)(2,1)S(1)} %collective-permute-done, ...), kind=kLoop, calls=%fused_computation.25 | loop fusion | flops 11796480 | bytes 4718592 | tf_op jit(solution)/shard_map/concatenate | solution.py:23
  90.4 0.0 copy-done.10
  90.4 5.8 %convolution_convert_fusion = bf16[2304,1536]{1,0:T(8,128)(2,1)} fusion(bf16[2304,512]{1,0:T(8,128)(2,1)S(1)} %bitcast.63, bf16[512,1536]{1,0:T(8,128)(2,1)S(1)} %copy-done.10), kind=kOutput, calls=%fused_computation.3 | convolution fusion | flops 3627417600 | bytes 11010048 | tf_op jit(solution)/shard_map/dot_general | solution.py:68
  96.3 18.0 %reshape.191 = bf16[4,3,8,3,8,3,8,64]{7,6,5,4,3,2,1,0:T(8,128)(2,1)} reshape(bf16[2304,1536]{1,0:T(8,128)(2,1)} %convolution_convert_fusion) | data formatting | bytes 14155776 | tf_op jit(solution)/shard_map/reshape | solution.py:71
  114.3 11.2 %copy.74 = bf16[4,3,3,8,8,3,8,64]{7,4,3,6,2,1,0,5:T(8,128)(2,1)} copy(bf16[4,3,3,8,8,3,8,64]{7,6,5,4,2,3,1,0:T(8,128)(2,1)} %bitcast.51) | data formatting | bytes 14155776 | tf_op jit(solution)/shard_map/transpose | solution.py:74
  125.5 6.4 %fusion.3 = f32[4,9,8,64,64]{3,4,2,1,0:T(8,128)S(1)} fusion(bf16[4,9,64,3,8,64]{5,2,4,1,0,3:T(8,128)(2,1)} %bitcast.49), kind=kOutput, calls=%fused_computation.11 | convolution fusion | flops 150994944 | bytes 14155776 | tf_op jit(solution)/shard_map/bwqhd,bwkhd->bwhqk/dot_general | solution.py:34
  131.8 5.4 %fusion.25 = (f32[4,9,8,64]{3,2,1,0:T(8,128)S(1)}, f32[4,9,8,64,64]{3,4,2,1,0:T(8,128)}) fusion(f32[4,9,8,64,64]{3,4,2,1,0:T(8,128)S(1)} %fusion.3, pred[9,64,64]{1,2,0:T(8,128)(4,1)S(1)} %broadcast_compare_fusion), kind=kOutput, calls=%fused_computation.76 | output fusion | flops 8257599 | bytes 9547776 | tf_op jit(solution)/shard_map/sub | solution.py:43
  137.2 9.2 %convert_bitcast_fusion = bf16[4,9,64,8,64]{2,4,3,1,0:T(8,128)(2,1)} fusion(f32[4,9,8,64,64]{3,4,2,1,0:T(8,128)} %get-tuple-element.12, f32[4,9,8,64]{3,2,1,0:T(8,128)S(1)} %get-tuple-element.11, bf16[4,9,64,3,8,64]{5,2,4,1,0,3:T(8,128)(2,1)} %bitcast.50), kind=kOutput, calls=%fused_computation.14 | convolution fusion | flops 154533888 | bytes 16588800 | tf_op jit(solution)/shard_map/bwhqk,bwkhd->bwqhd/dot_general | solution.py:45
  146.4 7.0 %copy.80 = bf16[4,9,64,8,64]{4,3,2,1,0:T(8,128)(2,1)} copy(bf16[4,9,64,8,64]{2,4,3,1,0:T(8,128)(2,1)} %convert_bitcast_fusion) | data formatting | bytes 4718592 | tf_op jit(solution)/shard_map/convert_element_type | solution.py:47
  153.4 7.4 %reshape.193 = bf16[4,3,3,8,8,512]{5,4,3,2,1,0:T(8,128)(2,1)} reshape(bf16[4,9,64,8,64]{4,3,2,1,0:T(8,128)(2,1)} %copy.80) | data formatting | bytes 4718592 | tf_op jit(solution)/shard_map/reshape | solution.py:91
  160.8 1.9 copy.81
  162.7 0.5 slice.41
  163.2 0.0 copy-start.5
  163.2 0.0 copy-start.11
  163.2 0.0 copy-done.4
  163.2 0.0 copy-done.6
  163.2 0.8 fusion.26
  164.0 0.4 multiply_reduce_fusion
  164.5 0.0 copy-done
  164.5 0.7 copy-done.5
  165.2 0.0 copy-done.11
  165.2 4.1 %add_convert_fusion = bf16[1024,1725]{0,1:T(8,128)(2,1)} fusion(bf16[1024,1725]{0,1:T(8,128)(2,1)S(1)} %copy-done.5, bf16[512,1725]{0,1:T(8,128)(2,1)S(1)} %copy-done, f32[1024,512]{1,0:T(8,128)S(1)} %get-tuple-element.14, f32[512]{0:T(512)S(1)} %copy-done.11, f32[1024]{0:T(1024)S(1)} %add_rsqrt_fusion, f32[1024]{0:T(1024)S(1)} %broadcast_multiply_fusion), kind=kOutput, calls=%fused_computation.8 | convolution fusion | flops 1816189952 | bytes 10939392 | tf_op jit(solution)/shard_map/dot_general | solution.py:101
  169.3 5.8 %copy.83 = bf16[1024,1725]{1,0:T(8,128)(2,1)} copy(bf16[1024,1725]{0,1:T(8,128)(2,1)} %add_convert_fusion) | data formatting | bytes 7065600 | tf_op jit(solution)/shard_map/convert_element_type | solution.py:102
  175.0 4.2 %copy.84 = bf16[4,4,4,1,16,1725]{5,4,2,0,3,1:T(8,128)(2,1)} copy(bf16[4,4,4,1,16,1725]{5,4,2,1,0,3:T(8,128)(2,1)} %bitcast.54) | data formatting | bytes 7065600 | tf_op jit(solution)/shard_map/reshape | solution.py:103
  179.3 4.9 %all-to-all-start.1 = ((bf16[4,4,4,1,16,1725]{5,4,2,0,3,1:T(8,128)(2,1)}), bf16[4,4,4,1,16,1725]{5,4,2,0,3,1:T(8,128)(2,1)}, u32[]{:S(2)}, u32[]{:S(2)}) async-start(bf16[4,4,4,1,16,1725]{5,4,2,0,3,1:T(8,128)(2,1)} %copy.84), calls=%async_computation.1 | async-start | bytes 7340032 | tf_op jit(solution)/shard_map/all_to_all | solution.py:104
  184.2 0.2 compare_reduce_fusion
  184.4 41.3 %all-to-all-done.1 = bf16[4,4,4,1,16,1725]{5,4,2,0,3,1:T(8,128)(2,1)} async-done(((bf16[4,4,4,1,16,1725]{5,4,2,0,3,1:T(8,128)(2,1)}), bf16[4,4,4,1,16,1725]{5,4,2,0,3,1:T(8,128)(2,1)}, u32[]{:S(2)}, u32[]{:S(2)}) %all-to-all-start.1) | async-done | bytes 3532832 | tf_op jit(solution)/shard_map/all_to_all | solution.py:104
  225.7 2.6 %copy.85 = bf16[4,4,4,1,16,1725]{5,4,1,2,0,3:T(8,128)(2,1)S(1)} copy(bf16[4,4,4,1,16,1725]{5,4,2,0,3,1:T(8,128)(2,1)} %all-to-all-done.1) | data formatting | bytes 7065600 | tf_op jit(solution)/shard_map/all_to_all | solution.py:104
  228.3 0.5 copy-done.2
  228.8 2.3 broadcast_select_fusion
  (22 shorter events, 0.1 us)
Async XLA Ops:
  0.0 164.5 %copy-start = (bf16[512,1725]{0,1:T(8,128)(2,1)S(1)}, bf16[512,1725]{0,1:T(8,128)(2,1)}, u32[]{:S(2)}) copy-start(bf16[512,1725]{0,1:T(8,128)(2,1)} %param.17) | copy-start | bytes 5299204
  4.4 4.9 %copy-start.7 = (s32[64,64]{1,0:T(8,128)S(1)}, s32[64,64]{1,0:T(8,128)}, u32[]{:S(2)}) copy-start(s32[64,64]{1,0:T(8,128)} %param.11) | copy-start | bytes 49156
  4.4 46.9 %all-to-all-start = ((bf16[4,1,4,4,16,1725]{5,4,2,0,1,3:T(8,128)(2,1)}), bf16[4,1,4,4,16,1725]{5,4,2,0,1,3:T(8,128)(2,1)}, u32[]{:S(2)}, u32[]{:S(2)}) async-start(bf16[4,1,4,4,16,1725]{5,4,2,0,1,3:T(8,128)(2,1)} %copy.71), calls=%async_computation | async-start | bytes 7340032 | tf_op jit(solution)/shard_map/all_to_all | solution.py:62
  51.4 2.6 %copy-start.9 = (bf16[1725,512]{1,0:T(8,128)(2,1)S(1)}, bf16[1725,512]{1,0:T(8,128)(2,1)}, u32[]{:S(2)}) copy-start(bf16[1725,512]{1,0:T(8,128)(2,1)} %param.12) | copy-start | bytes 5299204
  53.8 2.3 copy-start.1
  53.9 3.1 %copy-start.8 = (f32[512]{0:T(512)S(1)}, f32[512]{0:T(512)}, u32[]{:S(2)}) copy-start(f32[512]{0:T(512)} %param.13) | copy-start | bytes 6148
  56.1 1.0 copy-start.3
  58.3 10.6 %collective-permute-start = (bf16[4,4,16,512]{3,2,1,0:T(8,128)(2,1)}, bf16[4,4,16,512]{3,2,1,0:T(8,128)(2,1)S(1)}, u32[]{:S(2)}, u32[]{:S(2)}) collective-permute-start(bf16[4,4,16,512]{3,2,1,0:T(8,128)(2,1)} %get-tuple-element.7), channel_id=1, source_target_pairs={{0,8},{8,16},{16,24},{24,0},{1,9},{9,17},{17,25},{25,1},{2,10},{10... | collective-permute-start | bytes 786440 | tf_op jit(solution)/shard_map/ppermute | solution.py:21
  60.8 13.4 %collective-permute-start.1 = (bf16[4,4,16,512]{3,2,1,0:T(8,128)(2,1)}, bf16[4,4,16,512]{3,2,1,0:T(8,128)(2,1)S(1)}, u32[]{:S(2)}, u32[]{:S(2)}) collective-permute-start(bf16[4,4,16,512]{3,2,1,0:T(8,128)(2,1)} %get-tuple-element.8), channel_id=1, source_target_pairs={{8,0},{16,8},{24,16},{0,24},{9,1},{17,9},{25,17},{1,25},{10,2},{18... | collective-permute-start | bytes 786440 | tf_op jit(solution)/shard_map/ppermute | solution.py:22
  75.5 8.8 %collective-permute-start.2 = (bf16[4,24,4,512]{3,2,1,0:T(4,128)(2,1)}, bf16[4,24,4,512]{3,2,1,0:T(4,128)(2,1)}, u32[]{:S(2)}, u32[]{:S(2)}) collective-permute-start(bf16[4,24,4,512]{3,2,1,0:T(4,128)(2,1)} %get-tuple-element.5), channel_id=1, source_target_pairs={{0,2},{2,4},{4,6},{6,0},{1,3},{3,5},{5,7},{7,1},{8,10},{10,12},{12... | collective-permute-start | bytes 1179656 | tf_op jit(solution)/shard_map/ppermute | solution.py:21
  76.8 10.8 %collective-permute-start.3 = (bf16[4,24,4,512]{3,2,1,0:T(4,128)(2,1)}, bf16[4,24,4,512]{3,2,1,0:T(4,128)(2,1)}, u32[]{:S(2)}, u32[]{:S(2)}) collective-permute-start(bf16[4,24,4,512]{3,2,1,0:T(4,128)(2,1)} %get-tuple-element.6), channel_id=1, source_target_pairs={{2,0},{4,2},{6,4},{0,6},{3,1},{5,3},{7,5},{1,7},{10,8},{12,10},{14... | collective-permute-start | bytes 1179656 | tf_op jit(solution)/shard_map/ppermute | solution.py:22
  83.0 7.4 %copy-start.10 = (bf16[512,1536]{1,0:T(8,128)(2,1)S(1)}, bf16[512,1536]{1,0:T(8,128)(2,1)}, u32[]{:S(2)}) copy-start(bf16[512,1536]{1,0:T(8,128)(2,1)} %param.14) | copy-start | bytes 4718596
  160.8 2.5 %copy-start.4 = (bf16[1024,512]{1,0:T(8,128)(2,1)S(1)}, bf16[1024,512]{1,0:T(8,128)(2,1)}, u32[]{:S(2)}) copy-start(bf16[1024,512]{1,0:T(8,128)(2,1)} %copy-done.3) | copy-start | bytes 3145732
  160.8 2.5 %copy-start.6 = (bf16[512,512]{1,0:T(8,128)(2,1)S(1)}, bf16[512,512]{1,0:T(8,128)(2,1)}, u32[]{:S(2)}) copy-start(bf16[512,512]{1,0:T(8,128)(2,1)} %param.15) | copy-start | bytes 1572868
  163.2 2.0 copy-start.5
  163.2 2.0 copy-start.11
  179.3 4.9 %copy-start.12 = (s32[6]{0:T(128)S(1)}, s32[6]{0:T(128)}, u32[]{:S(2)}) copy-start(s32[6]{0:T(128)} %param.10) | copy-start | bytes 76
  179.3 46.4 %all-to-all-start.1 = ((bf16[4,4,4,1,16,1725]{5,4,2,0,3,1:T(8,128)(2,1)}), bf16[4,4,4,1,16,1725]{5,4,2,0,3,1:T(8,128)(2,1)}, u32[]{:S(2)}, u32[]{:S(2)}) async-start(bf16[4,4,4,1,16,1725]{5,4,2,0,3,1:T(8,128)(2,1)} %copy.84), calls=%async_computation.1 | async-start | bytes 7340032 | tf_op jit(solution)/shard_map/all_to_all | solution.py:104
  225.7 3.1 %copy-start.2 = (bf16[4,4,64,1725]{3,2,1,0:T(8,128)(2,1)S(1)}, bf16[4,4,64,1725]{3,2,1,0:T(8,128)(2,1)}, u32[]{:S(2)}) copy-start(bf16[4,4,64,1725]{3,2,1,0:T(8,128)(2,1)} %param.9) | copy-start | bytes 10598404
where the time goes:
time: 233 us; the launch traced here: 231 us
  waiting for transfers between devices  97.8 us (42%)
  local copies, waits for them, and re-layouts  75.5 us (32%)
  matrix products  28.4 us (12%)
  starting transfers between devices  15.7 us (7%)
  other arithmetic  13.5 us (6%)
    all_to_all x1, waiting for transfers between devices, local(): lax.all_to_all(local_rows, 'lon', split_axis=3, concat_axis=1, tiled=True)  41.3 us
    all_to_all x1, waiting for transfers between devices, local(): lax.all_to_all(outgoing, 'lon', split_axis=1, concat_axis=3, tiled=True)  41.3 us
    reshape x1, local copies, waits for them, and re-layouts, local(): projected.reshape(slots_here, ext_rows // WIN, WIN, ext_cols // WIN, WIN,...  18 us
    transpose x1, local copies, waits for them, and re-layouts, local(): windows.transpose(0, 1, 3, 2, 4, 5, 6, 7)  11.2 us
    dot_general x1, matrix products, window_mix(): jnp.einsum('bwhqk,bwkhd->bwqhd', weights, windows[:, :, :, 2], preferred_...  9.19 us
    ppermute x2, waiting for transfers between devices, with_halo(): after = lax.ppermute(leading, axis, down)  8.68 us
    reshape x1, local copies, waits for them, and re-layouts, local(): mixed_heads.reshape(slots_here, ext_rows // WIN, ext_cols // WIN, WIN, WI...  7.36 us
    convert_element_type x1, local copies, waits for them, and re-layouts, window_mix(): return jnp.einsum('bwhqk,bwkhd->bwqhd', weights, windows[:, :, :, 2], pre...  6.99 us
  transfers between devices with their start and end apart: 6, of which 6 were waited for; matrix products, arithmetic and copies ran while one was open for 3% of the time, Pallas kernels for 0%

commit v1 on v0

--- a/solution.py
+++ b/solution.py
@@ -1,14 +1,19 @@
+import functools
 import math
 
 import jax
 import jax.numpy as jnp
 from jax import lax
+from jax.experimental import pallas as pl
+from jax.experimental.pallas import tpu as pltpu
 from jax.sharding import PartitionSpec as P
 
 D = 512
 HEADS = 8
 HDIM = 64
 WIN = 8
+HALF = WIN // 2
+VMEM_LIMIT = 56 * 1024 * 1024
 
 
 def with_halo(array, sides, width):
@@ -47,7 +52,7 @@
     ).astype(jnp.bfloat16)
 
 
-def local(store, sample_index, region_ids, w_embed, attn_gain, w_qkv, w_out, out_gain, w_dec):
+def local_tiles(store, sample_index, region_ids, w_embed, attn_gain, w_qkv, w_out, out_gain, w_dec):
     lon_count = lax.axis_size("lon")
     slots_here, rows_here, width_all, patch_len = store.shape
     patch_cols = width_all // lon_count
@@ -106,6 +111,285 @@
     return jnp.where(occupied[:, None, None, None], strip_data, store)
 
 
+def to_windows(values):
+    rows, cols = HALF, values.shape[0] // HALF
+    parts = [pltpu.roll(values[cols * i : cols * (i + 1)], cols - HALF, 0) for i in range(rows)]
+    return jnp.concatenate(
+        [parts[i][WIN * c : WIN * (c + 1)] for c in range(cols // WIN) for i in range(rows)], axis=0
+    )
+
+
+def from_windows(values):
+    rows, cols = HALF, values.shape[0] // HALF
+    parts = []
+    for i in range(rows):
+        line = jnp.concatenate(
+            [
+                values[WIN * (rows * c + i) : WIN * (rows * c + i + 1)]
+                for c in range(cols // WIN)
+            ],
+            axis=0,
+        )
+        parts.append(pltpu.roll(line, HALF, 0))
+    return jnp.concatenate(parts, axis=0)
+
+
+def embed_slot(patches, w_embed, gain):
+    embedded = jnp.dot(patches, w_embed, preferred_element_type=jnp.float32).astype(jnp.bfloat16)
+    embedded = to_windows(embedded.astype(jnp.float32))
+    normed = layer_norm(embedded, gain).astype(jnp.bfloat16)
+    return embedded.astype(jnp.bfloat16), normed
+
+
+NT = (((1,), (1,)), ((), ()))
+TN = (((0,), (0,)), ((), ()))
+GROUP = 4
+WIDE = GROUP * HDIM
+PER = WIN * HALF
+
+
+def attend_slot(query, kv_own, kv_other, q_regions, k_regions):
+    shape = (GROUP * PER, WIDE)
+    pick = (
+        lax.broadcasted_iota(jnp.int32, shape, 0) // PER
+        == lax.broadcasted_iota(jnp.int32, shape, 1) // HDIM
+    )
+    head_mask = jnp.where(pick, 1.0, 0.0).astype(jnp.bfloat16)
+    windows = query.shape[0] // PER
+    kvs, scores, weights, mixed = [], [], [], []
+    for c in range(windows):
+        at = slice(PER * c, PER * (c + 1))
+        kvs.append(jnp.concatenate([kv_own[at], kv_other[at]], axis=0))
+        for g in range(HEADS // GROUP):
+            cols = slice(WIDE * g, WIDE * (g + 1))
+            queries = jnp.concatenate([query[at, cols]] * GROUP, axis=0) * head_mask
+            scores.append(
+                lax.dot_general(kvs[c][:, cols], queries, NT, preferred_element_type=jnp.float32)
+            )
+    for c in range(windows):
+        seen = k_regions[:, c : c + 1] == q_regions[c : c + 1, :]
+        for g in range(HEADS // GROUP):
+            part = jnp.where(seen, scores[2 * c + g], -1e30)
+            expo = jnp.exp(part - jnp.max(part, axis=0, keepdims=True))
+            total = jnp.sum(expo, axis=0, keepdims=True)
+            weights.append((expo * (1.0 / total)).astype(jnp.bfloat16))
+    for c in range(windows):
+        groups = []
+        for g in range(HEADS // GROUP):
+            heads = lax.dot_general(
+                weights[2 * c + g],
+                kvs[c][:, D + WIDE * g : D + WIDE * (g + 1)],
+                TN,
+                preferred_element_type=jnp.float32,
+            )
+            heads = jnp.where(pick, heads, 0.0)
+            total = heads[:PER]
+            for h in range(1, GROUP):
+                total = total + heads[PER * h : PER * (h + 1)]
+            groups.append(total)
+        mixed.append(jnp.concatenate(groups, axis=1).astype(jnp.bfloat16))
+    return jnp.concatenate(mixed, axis=0)
+
+
+def region_tables(own, far):
+    rows, cols = own.shape
+    windows = cols // WIN
+    lines = [own[i : i + 1] for i in range(rows)] + [far[i : i + 1] for i in range(rows)]
+    wide = jnp.concatenate([jnp.broadcast_to(line, (WIN, cols)) for line in lines], axis=0)
+    row = lax.broadcasted_iota(jnp.int32, wide.shape, 0)
+    col = lax.broadcasted_iota(jnp.int32, wide.shape, 1)
+    kept = jnp.where((col + WIN - HALF) % WIN == row % WIN, wide, 0.0).astype(jnp.bfloat16)
+    place = (lax.broadcasted_iota(jnp.int32, (windows, cols), 1) + cols - HALF) % cols // WIN
+    here = place == lax.broadcasted_iota(jnp.int32, (windows, cols), 0)
+    here = jnp.where(here, 1.0, 0.0).astype(jnp.bfloat16)
+    k_regions = lax.dot_general(kept, here, NT, preferred_element_type=jnp.float32)
+    q_rows = jnp.concatenate([kept[:PER]] * GROUP, axis=0)
+    q_regions = lax.dot_general(here, q_rows, NT, preferred_element_type=jnp.float32)
+    return q_regions, k_regions
+
+
+def finish_slot(embedded, mixed, w_out, gain):
+    updated = embedded.astype(jnp.float32) + jnp.dot(
+        mixed, w_out, preferred_element_type=jnp.float32
+    )
+    return from_windows(layer_norm(updated, gain)).astype(jnp.bfloat16)
+
+
+def decode_slot(patches, final, w_dec_t):
+    return (
+        patches.astype(jnp.float32)
+        + lax.dot_general(
+            final, w_dec_t, (((1,), (1,)), ((), ())), preferred_element_type=jnp.float32
+        )
+    ).astype(jnp.bfloat16)
+
+
+def fused_kernel(
+    sample_ref,
+    region_ref,
+    a_gain_ref,
+    o_gain_ref,
+    store_ref,
+    w_embed_ref,
+    w_qkv_ref,
+    w_out_ref,
+    w_dec_ref,
+    new_ref,
+    patches,
+    w_embed,
+    w_qkv,
+    w_out,
+    w_dec,
+    embedded,
+    own,
+    far,
+    own_qkv,
+    slot_sems,
+    weight_sems,
+    out_sems,
+    send_sems,
+    recv_sems,
+):
+    slots, rows_here, cols, patch_len = store_ref.shape
+    lon_count = lax.axis_size("lon")
+    strips = lax.axis_size("lat") * lon_count
+    mine = lax.axis_index("lat") * lon_count + lax.axis_index("lon")
+    other = lax.rem(mine + 2 * lax.rem(mine, 2) - 1 + strips, strips)
+    partner = {"lat": lax.div(other, lon_count), "lon": lax.rem(other, lon_count)}
+
+    def slot_in(s):
+        return pltpu.make_async_copy(store_ref.at[s], patches.at[s], slot_sems.at[s])
+
+    def slot_out(s):
+        return pltpu.make_async_copy(patches.at[s], new_ref.at[s], out_sems.at[s])
+
+    def send(s):
+        return pltpu.make_async_remote_copy(
+            src_ref=own.at[s],
+            dst_ref=far.at[s],
+            send_sem=send_sems.at[s],
+            recv_sem=recv_sems.at[s],
+            device_id=partner,
+            device_id_type=pl.DeviceIdType.MESH,
+        )
+
+    weights = [
+        pltpu.make_async_copy(src, dst, weight_sems.at[i])
+        for i, (src, dst) in enumerate(
+            ((w_embed_ref, w_embed), (w_qkv_ref, w_qkv), (w_out_ref, w_out), (w_dec_ref, w_dec))
+        )
+    ]
+    slot_in(0).start()
+    weights[0].start()
+    for s in range(1, slots):
+        slot_in(s).start()
+    for copy in weights[1:]:
+        copy.start()
+
+    barrier = pltpu.get_barrier_semaphore()
+    pl.semaphore_signal(
+        barrier, inc=1, device_id=partner, device_id_type=pl.DeviceIdType.MESH
+    )
+    q_regions, k_regions = region_tables(
+        region_ref[pl.ds(mine * HALF, HALF), :].astype(jnp.float32),
+        region_ref[pl.ds(other * HALF, HALF), :].astype(jnp.float32),
+    )
+    pl.semaphore_wait(barrier, 1)
+    weights[0].wait()
+
+    @pl.loop(0, slots)
+    def _(s):
+        slot_in(s).wait()
+        flat = patches[s].reshape(rows_here * cols, patch_len)
+        embedded[s], own[s] = embed_slot(flat, w_embed[...], a_gain_ref[...])
+        send(s).start()
+
+    weights[1].wait()
+
+    @pl.loop(0, slots)
+    def _(s):
+        query = jnp.dot(own[s], w_qkv[:, :D], preferred_element_type=jnp.float32)
+        own_qkv[s, :, :D] = (query * (1.0 / math.sqrt(HDIM))).astype(jnp.bfloat16)
+        own_qkv[s, :, D:] = jnp.dot(
+            own[s], w_qkv[:, D:], preferred_element_type=jnp.float32
+        ).astype(jnp.bfloat16)
+
+    weights[2].wait()
+    weights[3].wait()
+
+    @pl.loop(0, slots)
+    def _(s):
+        send(s).wait()
+        kv_other = jnp.dot(far[s], w_qkv[:, D:], preferred_element_type=jnp.float32)
+        mixed = attend_slot(
+            own_qkv[s, :, :D],
+            own_qkv[s, :, D:],
+            kv_other.astype(jnp.bfloat16),
+            q_regions,
+            k_regions,
+        )
+        final = finish_slot(embedded[s], mixed, w_out[...], o_gain_ref[...])
+        slot = lax.axis_index("buf") * slots + s
+        taken = sample_ref[0] == slot
+        for b in range(1, sample_ref.shape[0]):
+            taken = jnp.logical_or(taken, sample_ref[b] == slot)
+        final = jnp.where(taken, final, jnp.zeros_like(final))
+        flat = patches[s].reshape(rows_here * cols, patch_len)
+        patches[s] = decode_slot(flat, final, w_dec[...]).reshape(rows_here, cols, patch_len)
+        slot_out(s).start()
+
+    @pl.loop(0, slots)
+    def _(s):
+        slot_out(s).wait()
+
+
+def local_strips(store, sample_index, region_ids, w_embed, attn_gain, w_qkv, w_out, out_gain, w_dec):
+    slots, rows_here, cols, patch_len = store.shape
+    tokens = rows_here * cols
+    held = lambda *shape: pltpu.VMEM(shape, jnp.bfloat16)
+    vmem = pl.BlockSpec(memory_space=pltpu.VMEM)
+    hbm = pl.BlockSpec(memory_space=pl.ANY)
+    return pl.pallas_call(
+        fused_kernel,
+        in_specs=[pl.BlockSpec(memory_space=pltpu.SMEM), vmem, vmem, vmem] + [hbm] * 5,
+        out_specs=hbm,
+        out_shape=jax.ShapeDtypeStruct(store.shape, store.dtype),
+        scratch_shapes=[
+            held(*store.shape),
+            held(*w_embed.shape),
+            held(*w_qkv.shape),
+            held(*w_out.shape),
+            held(*w_dec.shape[::-1]),
+            held(slots, tokens, D),
+            held(slots, tokens, D),
+            held(slots, tokens, D),
+            held(slots, tokens, 3 * D),
+            pltpu.SemaphoreType.DMA((slots,)),
+            pltpu.SemaphoreType.DMA((4,)),
+            pltpu.SemaphoreType.DMA((slots,)),
+            pltpu.SemaphoreType.DMA((slots,)),
+            pltpu.SemaphoreType.DMA((slots,)),
+        ],
+        compiler_params=pltpu.CompilerParams(
+            vmem_limit_bytes=VMEM_LIMIT, collective_id=0, has_side_effects=True
+        ),
+    )(
+        sample_index,
+        region_ids,
+        attn_gain[None],
+        out_gain[None],
+        store,
+        w_embed,
+        w_qkv,
+        w_out,
+        w_dec.T,
+    )
+
+
+def local(store, *rest):
+    return (local_strips if store.shape[1] == HALF else local_tiles)(store, *rest)
+
+
 def solution(mesh):
     return jax.shard_map(
         local,

time: 233 us -> 37.5 us (0.16)
  waiting for transfers between devices: 97.8 us -> 0 us
  local copies, waits for them, and re-layouts: 75.5 us -> 4.22 us
  Pallas kernels: 0 us -> 33.1 us
  matrix products: 28.4 us -> 0 us
  starting transfers between devices: 15.7 us -> 0 us
  other arithmetic: 13.5 us -> 0 us
    all_to_all x2 -> x0, waiting for transfers between devices: 82.6 us -> none  [the longest x1 41.3 us: local(): lax.all_to_all(local_rows, 'lon', split_axis=3, concat_axis=1, tiled=True)]
    reshape x5 -> x0, local copies, waits for them, and re-layouts: 39.9 us -> none  [the longest x1 18 us: local(): projected.reshape(slots_here, ext_rows // WIN, WIN, ext_cols // WIN, WIN,...]
    pallas_call x0 -> x1, Pallas kernels: none -> 33.1 us  [local_strips(): pl.pallas_call(fused_kernel, in_specs=[pl.BlockSpec(memory_space=pltpu.SM...]
    dot_general x6 -> x0, matrix products: 28.4 us -> none  [the longest x1 9.19 us: window_mix(): jnp.einsum('bwhqk,bwkhd->bwqhd', weights, windows[:, :, :, 2], preferred_...]
    ppermute x4 -> x0, waiting for transfers between devices: 15.2 us -> none  [the longest x2 8.68 us: with_halo(): after = lax.ppermute(leading, axis, down)]
    transpose x3 -> x0, local copies, waits for them, and re-layouts: 13.1 us -> none  [the longest x1 11.2 us: local(): windows.transpose(0, 1, 3, 2, 4, 5, 6, 7)]
    convert_element_type x2 -> x0, local copies, waits for them, and re-layouts: 12.8 us -> none  [the longest x1 6.99 us: window_mix(): return jnp.einsum('bwhqk,bwkhd->bwqhd', weights, windows[:, :, :, 2], pre...]
    all_to_all x2 -> x0, starting transfers between devices: 9.79 us -> none  [the longest x1 4.9 us: local(): lax.all_to_all(local_rows, 'lon', split_axis=3, concat_axis=1, tiled=True)]
  transfers between devices with their start and end apart: 6 -> 0, of which waited for: 6 -> 0; matrix products, arithmetic and copies ran while one was open for 3% -> 0% of each run, Pallas kernels for 0% -> 0%
where the time goes in v1:
time: 37.5 us; the launch traced here: 37.3 us
  Pallas kernels  33.1 us (88%)
  local copies, waits for them, and re-layouts  4.22 us (11%)
    pallas_call x1, Pallas kernels, local_strips(): pl.pallas_call(fused_kernel, in_specs=[pl.BlockSpec(memory_space=pltpu.SM...  33.1 us
    unnamed x1, local copies, waits for them, and re-layouts  4.22 us

profile of v1, /device:TPU:1, one launch (start us, length us, event | category | flops | bytes accessed | tf_op | source)
XLA Modules:
  0.0 37.3 jit_solution(2168542035257098668)
XLA Ops:
  0.0 33.1 %shard_map.91 = bf16[4,4,64,1725]{3,2,1,0:T(8,128)(2,1)} custom-call(s32[6]{0:T(128)} %sample_ref.1, s32[64,64]{1,0:T(8,128)} %region_ref.1, f32[1,512]{1,0:T(1,128)} %bitcast.4, f32[1,512]{1,0:T(1,128)} %bitcast.5, bf16[4,4,64,1725]{3,2,1,0:T(8,128)(2,1)} %store_ref.1, bf16[1725,512]{1,0:T(8,128)(2,1)} %w_embed_ref.1, bf16[512,1536]{1,0:T(8,128)(2,1)} %w_qkv_ref.1, ...), custom_call_target="tpu_custom_call" | custom-call | tf_op jit(solution)/shard_map/pallas_call | solution.py:352
  33.1 4.2 %copy.11 = bf16[4,4,64,1725]{3,2,1,0:T(8,128)(2,1)} copy(bf16[4,4,64,1725]{3,2,1,0:T(8,128)(2,1)} %shard_map.91) | data formatting | bytes 7065600

commit v2 on v1

--- a/solution.py
+++ b/solution.py
@@ -14,6 +14,7 @@
 WIN = 8
 HALF = WIN // 2
 VMEM_LIMIT = 56 * 1024 * 1024
+PICK_LIMIT = 4 * 1024 * 1024
 
 
 def with_halo(array, sides, width):
@@ -208,11 +209,11 @@
     return q_regions, k_regions
 
 
-def finish_slot(embedded, mixed, w_out, gain):
+def finish_part(embedded, mixed, w_out, gain):
     updated = embedded.astype(jnp.float32) + jnp.dot(
         mixed, w_out, preferred_element_type=jnp.float32
     )
-    return from_windows(layer_norm(updated, gain)).astype(jnp.bfloat16)
+    return layer_norm(updated, gain)
 
 
 def decode_slot(patches, final, w_dec_t):
@@ -224,7 +225,20 @@
     ).astype(jnp.bfloat16)
 
 
+def taken_slots(sample_ref, slots):
+    first = lax.axis_index("buf") * slots
+    taken = []
+    for s in range(slots):
+        found = sample_ref[0] == first + s
+        for b in range(1, sample_ref.shape[0]):
+            found = jnp.logical_or(found, sample_ref[b] == first + s)
+        taken.append(jnp.where(found, 1, 0))
+    ranks = [sum(taken[:s], jnp.int32(0)) for s in range(slots)]
+    return taken, ranks
+
+
 def fused_kernel(
+    count,
     sample_ref,
     region_ref,
     a_gain_ref,
@@ -244,6 +258,8 @@
     own,
     far,
     own_qkv,
+    finals,
+    result,
     slot_sems,
     weight_sems,
     out_sems,
@@ -261,14 +277,18 @@
         return pltpu.make_async_copy(store_ref.at[s], patches.at[s], slot_sems.at[s])
 
     def slot_out(s):
-        return pltpu.make_async_copy(patches.at[s], new_ref.at[s], out_sems.at[s])
-
-    def send(s):
+        return pltpu.make_async_copy(result.at[s], new_ref.at[s], out_sems.at[s])
+
+    tokens = rows_here * cols
+    half = tokens // 2
+    halves = [pl.ds(half * h, half) for h in range(2)]
+
+    def send(k, h):
         return pltpu.make_async_remote_copy(
-            src_ref=own.at[s],
-            dst_ref=far.at[s],
-            send_sem=send_sems.at[s],
-            recv_sem=recv_sems.at[s],
+            src_ref=own.at[k, halves[h]],
+            dst_ref=far.at[k, halves[h]],
+            send_sem=send_sems.at[k, h],
+            recv_sem=recv_sems.at[k, h],
             device_id=partner,
             device_id_type=pl.DeviceIdType.MESH,
         )
@@ -295,83 +315,123 @@
         region_ref[pl.ds(other * HALF, HALF), :].astype(jnp.float32),
     )
     pl.semaphore_wait(barrier, 1)
+    compact = count < slots
+    taken, ranks = taken_slots(sample_ref, slots)
+
+    def slot_of(k):
+        if not compact:
+            return k
+        slot = jnp.int32(0)
+        for s in range(slots):
+            slot += jnp.where(jnp.logical_and(taken[s] == 1, ranks[s] == k), s, 0)
+        return slot
+
     weights[0].wait()
-
-    @pl.loop(0, slots)
-    def _(s):
-        slot_in(s).wait()
-        flat = patches[s].reshape(rows_here * cols, patch_len)
-        embedded[s], own[s] = embed_slot(flat, w_embed[...], a_gain_ref[...])
-        send(s).start()
+    if compact:
+        for s in range(slots):
+            slot_in(s).wait()
+
+    @pl.loop(0, count)
+    def _(k):
+        if not compact:
+            slot_in(k).wait()
+        flat = patches[slot_of(k)].reshape(tokens, patch_len)
+        embedded[k], own[k] = embed_slot(flat, w_embed[...], a_gain_ref[...])
+        for h in range(2):
+            send(k, h).start()
 
     weights[1].wait()
 
-    @pl.loop(0, slots)
-    def _(s):
-        query = jnp.dot(own[s], w_qkv[:, :D], preferred_element_type=jnp.float32)
-        own_qkv[s, :, :D] = (query * (1.0 / math.sqrt(HDIM))).astype(jnp.bfloat16)
-        own_qkv[s, :, D:] = jnp.dot(
-            own[s], w_qkv[:, D:], preferred_element_type=jnp.float32
+    @pl.loop(0, count)
+    def _(k):
+        query = jnp.dot(own[k], w_qkv[:, :D], preferred_element_type=jnp.float32)
+        own_qkv[k, :, :D] = (query * (1.0 / math.sqrt(HDIM))).astype(jnp.bfloat16)
+        own_qkv[k, :, D:] = jnp.dot(
+            own[k], w_qkv[:, D:], preferred_element_type=jnp.float32
         ).astype(jnp.bfloat16)
 
     weights[2].wait()
     weights[3].wait()
-
-    @pl.loop(0, slots)
-    def _(s):
-        send(s).wait()
-        kv_other = jnp.dot(far[s], w_qkv[:, D:], preferred_element_type=jnp.float32)
-        mixed = attend_slot(
-            own_qkv[s, :, :D],
-            own_qkv[s, :, D:],
-            kv_other.astype(jnp.bfloat16),
-            q_regions,
-            k_regions,
-        )
-        final = finish_slot(embedded[s], mixed, w_out[...], o_gain_ref[...])
-        slot = lax.axis_index("buf") * slots + s
-        taken = sample_ref[0] == slot
-        for b in range(1, sample_ref.shape[0]):
-            taken = jnp.logical_or(taken, sample_ref[b] == slot)
-        final = jnp.where(taken, final, jnp.zeros_like(final))
-        flat = patches[s].reshape(rows_here * cols, patch_len)
-        patches[s] = decode_slot(flat, final, w_dec[...]).reshape(rows_here, cols, patch_len)
-        slot_out(s).start()
-
-    @pl.loop(0, slots)
-    def _(s):
-        slot_out(s).wait()
-
-
-def local_strips(store, sample_index, region_ids, w_embed, attn_gain, w_qkv, w_out, out_gain, w_dec):
+    windows = tokens // PER
+
+    @pl.loop(0, count)
+    def _(k):
+        for h in range(2):
+            send(k, h).wait()
+            at = slice(half * h, half * (h + 1))
+            here = slice(windows // 2 * h, windows // 2 * (h + 1))
+            kv_other = jnp.dot(far[k, at], w_qkv[:, D:], preferred_element_type=jnp.float32)
+            mixed = attend_slot(
+                own_qkv[k, at, :D],
+                own_qkv[k, at, D:],
+                kv_other.astype(jnp.bfloat16),
+                q_regions[here],
+                k_regions[:, here],
+            )
+            finals[at] = finish_part(embedded[k, at], mixed, w_out[...], o_gain_ref[...])
+        final = from_windows(finals[...]).astype(jnp.bfloat16)
+        flat = patches[slot_of(k)].reshape(tokens, patch_len)
+        result[k] = decode_slot(flat, final, w_dec[...]).reshape(rows_here, cols, patch_len)
+        slot_out(k).start()
+
+    @pl.loop(0, count)
+    def _(k):
+        slot_out(k).wait()
+
+
+def pick_kernel(sample_ref, result_ref, store_ref, new_ref, sems):
+    slots = store_ref.shape[0]
+    compact = result_ref.shape[0] < slots
+    taken, ranks = taken_slots(sample_ref, slots)
+    for s in range(slots):
+
+        @pl.when(taken[s] == 1)
+        def _():
+            source = result_ref.at[ranks[s] if compact else s]
+            pltpu.make_async_copy(source, new_ref.at[s], sems.at[s]).start()
+
+        @pl.when(taken[s] == 0)
+        def _():
+            pltpu.make_async_copy(store_ref.at[s], new_ref.at[s], sems.at[s]).start()
+
+    for s in range(slots):
+        pltpu.make_async_copy(store_ref.at[s], new_ref.at[s], sems.at[s]).wait()
+
+
+def strips_step(
+    count, store, sample_index, region_ids, w_embed, attn_gain, w_qkv, w_out, out_gain, w_dec
+):
     slots, rows_here, cols, patch_len = store.shape
     tokens = rows_here * cols
     held = lambda *shape: pltpu.VMEM(shape, jnp.bfloat16)
     vmem = pl.BlockSpec(memory_space=pltpu.VMEM)
     hbm = pl.BlockSpec(memory_space=pl.ANY)
-    return pl.pallas_call(
-        fused_kernel,
-        in_specs=[pl.BlockSpec(memory_space=pltpu.SMEM), vmem, vmem, vmem] + [hbm] * 5,
+    smem = pl.BlockSpec(memory_space=pltpu.SMEM)
+    result = pl.pallas_call(
+        functools.partial(fused_kernel, count),
+        in_specs=[smem, vmem, vmem, vmem] + [hbm] * 5,
         out_specs=hbm,
-        out_shape=jax.ShapeDtypeStruct(store.shape, store.dtype),
+        out_shape=pltpu.VMEM((count, *store.shape[1:]), store.dtype),
         scratch_shapes=[
             held(*store.shape),
             held(*w_embed.shape),
             held(*w_qkv.shape),
             held(*w_out.shape),
             held(*w_dec.shape[::-1]),
-            held(slots, tokens, D),
-            held(slots, tokens, D),
-            held(slots, tokens, D),
-            held(slots, tokens, 3 * D),
+            held(count, tokens, D),
+            held(count, tokens, D),
+            held(count, tokens, D),
+            held(count, tokens, 3 * D),
+            pltpu.VMEM((tokens, D), jnp.float32),
+            held(count, *store.shape[1:]),
             pltpu.SemaphoreType.DMA((slots,)),
             pltpu.SemaphoreType.DMA((4,)),
-            pltpu.SemaphoreType.DMA((slots,)),
-            pltpu.SemaphoreType.DMA((slots,)),
-            pltpu.SemaphoreType.DMA((slots,)),
+            pltpu.SemaphoreType.DMA((count,)),
+            pltpu.SemaphoreType.DMA((count, 2)),
+            pltpu.SemaphoreType.DMA((count, 2)),
         ],
         compiler_params=pltpu.CompilerParams(
-            vmem_limit_bytes=VMEM_LIMIT, collective_id=0, has_side_effects=True
+            vmem_limit_bytes=VMEM_LIMIT, collective_id=slots - count, has_side_effects=True
         ),
     )(
         sample_index,
@@ -384,6 +444,18 @@
         w_out,
         w_dec.T,
     )
+    return pl.pallas_call(
+        pick_kernel,
+        in_specs=[smem, hbm, hbm],
+        out_specs=hbm,
+        out_shape=jax.ShapeDtypeStruct(store.shape, store.dtype),
+        scratch_shapes=[pltpu.SemaphoreType.DMA((slots,))],
+        compiler_params=pltpu.CompilerParams(vmem_limit_bytes=PICK_LIMIT),
+    )(sample_index, result, store)
+
+
+def local_strips(store, *rest):
+    return strips_step(store.shape[0], store, *rest)
 
 
 def local(store, *rest):

time: 37.5 us -> 35.8 us (0.955)
  local copies, waits for them, and re-layouts: 4.22 us -> 0.01 us
  Pallas kernels: 33.1 us -> 35.6 us
    unnamed x1 -> x4, local copies, waits for them, and re-layouts: 4.22 us -> 0.01 us
    pallas_call x1 -> x2, Pallas kernels: 33.1 us -> 35.6 us  [the longest x1 33.2 us: strips_step(): pl.pallas_call(functools.partial(fused_kernel, count), in_specs=[smem, vm...]
where the time goes in v2:
time: 35.8 us; the launch traced here: 35.6 us
  Pallas kernels  35.6 us (99%)
    pallas_call x1, Pallas kernels, strips_step(): pl.pallas_call(functools.partial(fused_kernel, count), in_specs=[smem, vm...  33.2 us
    pallas_call x1, Pallas kernels, strips_step(): pl.pallas_call(pick_kernel, in_specs=[smem, hbm, hbm], out_specs=hbm, out...  2.42 us

profile of v2, /device:TPU:1, one launch (start us, length us, event | category | flops | bytes accessed | tf_op | source)
XLA Modules:
  0.0 35.6 jit_solution(2795999341715738862)
XLA Ops:
  0.0 0.0 copy-start
  0.0 0.0 copy-start.1
  0.0 33.2 %shard_map.91.result_ref = bf16[4,4,64,1725]{3,2,1,0:T(8,128)(2,1)S(1)} custom-call(s32[6]{0:T(128)} %sample_ref.3, s32[64,64]{1,0:T(8,128)} %region_ref.1, f32[1,512]{1,0:T(1,128)} %bitcast.4, f32[1,512]{1,0:T(1,128)} %bitcast.5, bf16[4,4,64,1725]{3,2,1,0:T(8,128)(2,1)} %store_ref.3, bf16[1725,512]{1,0:T(8,128)(2,1)} %w_embed_ref.1, ...), custom_call_target="tpu_custom_call" | custom-call | tf_op jit(solution)/shard_map/pallas_call | solution.py:410
  33.2 0.0 copy-done
  33.2 0.0 copy-done.1
  33.2 2.4 %shard_map.92 = bf16[4,4,64,1725]{3,2,1,0:T(8,128)(2,1)} custom-call(s32[6]{0:T(128)S(1)} %copy-done.1, bf16[4,4,64,1725]{3,2,1,0:T(8,128)(2,1)S(1)} %shard_map.91.result_ref, bf16[4,4,64,1725]{3,2,1,0:T(8,128)(2,1)S(1)} %copy-done), custom_call_target="tpu_custom_call" | custom-call | tf_op jit(solution)/shard_map/pallas_call | solution.py:447
Async XLA Ops:
  0.0 33.2 %copy-start = (bf16[4,4,64,1725]{3,2,1,0:T(8,128)(2,1)S(1)}, bf16[4,4,64,1725]{3,2,1,0:T(8,128)(2,1)}, u32[]{:S(2)}) copy-start(bf16[4,4,64,1725]{3,2,1,0:T(8,128)(2,1)} %store_ref.3) | copy-start | bytes 10598404
  0.0 33.2 %copy-start.1 = (s32[6]{0:T(128)S(1)}, s32[6]{0:T(128)}, u32[]{:S(2)}) copy-start(s32[6]{0:T(128)} %sample_ref.3) | copy-start | bytes 76

commit v3 on v1

--- a/solution.py
+++ b/solution.py
@@ -1,4 +1,3 @@
-import functools
 import math
 
 import jax
@@ -14,6 +13,7 @@
 WIN = 8
 HALF = WIN // 2
 VMEM_LIMIT = 56 * 1024 * 1024
+PICK_LIMIT = 4 * 1024 * 1024
 
 
 def with_halo(array, sides, width):
@@ -208,11 +208,11 @@
     return q_regions, k_regions
 
 
-def finish_slot(embedded, mixed, w_out, gain):
+def finish_part(embedded, mixed, w_out, gain):
     updated = embedded.astype(jnp.float32) + jnp.dot(
         mixed, w_out, preferred_element_type=jnp.float32
     )
-    return from_windows(layer_norm(updated, gain)).astype(jnp.bfloat16)
+    return layer_norm(updated, gain)
 
 
 def decode_slot(patches, final, w_dec_t):
@@ -244,9 +244,9 @@
     own,
     far,
     own_qkv,
+    finals,
     slot_sems,
     weight_sems,
-    out_sems,
     send_sems,
     recv_sems,
 ):
@@ -260,15 +260,16 @@
     def slot_in(s):
         return pltpu.make_async_copy(store_ref.at[s], patches.at[s], slot_sems.at[s])
 
-    def slot_out(s):
-        return pltpu.make_async_copy(patches.at[s], new_ref.at[s], out_sems.at[s])
-
-    def send(s):
+    tokens = rows_here * cols
+    half = tokens // 2
+    halves = [pl.ds(half * h, half) for h in range(2)]
+
+    def send(k, h):
         return pltpu.make_async_remote_copy(
-            src_ref=own.at[s],
-            dst_ref=far.at[s],
-            send_sem=send_sems.at[s],
-            recv_sem=recv_sems.at[s],
+            src_ref=own.at[k, halves[h]],
+            dst_ref=far.at[k, halves[h]],
+            send_sem=send_sems.at[k, h],
+            recv_sem=recv_sems.at[k, h],
             device_id=partner,
             device_id_type=pl.DeviceIdType.MESH,
         )
@@ -279,81 +280,101 @@
             ((w_embed_ref, w_embed), (w_qkv_ref, w_qkv), (w_out_ref, w_out), (w_dec_ref, w_dec))
         )
     ]
+    weights[0].start()
     slot_in(0).start()
-    weights[0].start()
+
+    barrier = pltpu.get_barrier_semaphore()
+    pl.semaphore_signal(
+        barrier, inc=1, device_id=partner, device_id_type=pl.DeviceIdType.MESH
+    )
+    q_regions, k_regions = region_tables(
+        region_ref[pl.ds(mine * HALF, HALF), :].astype(jnp.float32),
+        region_ref[pl.ds(other * HALF, HALF), :].astype(jnp.float32),
+    )
+    pl.semaphore_wait(barrier, 1)
+    weights[0].wait()
+    slot_in(0).wait()
     for s in range(1, slots):
         slot_in(s).start()
     for copy in weights[1:]:
         copy.start()
 
-    barrier = pltpu.get_barrier_semaphore()
-    pl.semaphore_signal(
-        barrier, inc=1, device_id=partner, device_id_type=pl.DeviceIdType.MESH
-    )
-    q_regions, k_regions = region_tables(
-        region_ref[pl.ds(mine * HALF, HALF), :].astype(jnp.float32),
-        region_ref[pl.ds(other * HALF, HALF), :].astype(jnp.float32),
-    )
-    pl.semaphore_wait(barrier, 1)
-    weights[0].wait()
-
     @pl.loop(0, slots)
-    def _(s):
-        slot_in(s).wait()
-        flat = patches[s].reshape(rows_here * cols, patch_len)
-        embedded[s], own[s] = embed_slot(flat, w_embed[...], a_gain_ref[...])
-        send(s).start()
+    def _(k):
+        @pl.when(k > 0)
+        def _():
+            slot_in(k).wait()
+
+        flat = patches[k].reshape(tokens, patch_len)
+        embedded[k], own[k] = embed_slot(flat, w_embed[...], a_gain_ref[...])
+        for h in range(2):
+            send(k, h).start()
 
     weights[1].wait()
 
     @pl.loop(0, slots)
-    def _(s):
-        query = jnp.dot(own[s], w_qkv[:, :D], preferred_element_type=jnp.float32)
-        own_qkv[s, :, :D] = (query * (1.0 / math.sqrt(HDIM))).astype(jnp.bfloat16)
-        own_qkv[s, :, D:] = jnp.dot(
-            own[s], w_qkv[:, D:], preferred_element_type=jnp.float32
+    def _(k):
+        query = jnp.dot(own[k], w_qkv[:, :D], preferred_element_type=jnp.float32)
+        own_qkv[k, :, :D] = (query * (1.0 / math.sqrt(HDIM))).astype(jnp.bfloat16)
+        own_qkv[k, :, D:] = jnp.dot(
+            own[k], w_qkv[:, D:], preferred_element_type=jnp.float32
         ).astype(jnp.bfloat16)
 
     weights[2].wait()
     weights[3].wait()
+    windows = tokens // PER
 
     @pl.loop(0, slots)
-    def _(s):
-        send(s).wait()
-        kv_other = jnp.dot(far[s], w_qkv[:, D:], preferred_element_type=jnp.float32)
-        mixed = attend_slot(
-            own_qkv[s, :, :D],
-            own_qkv[s, :, D:],
-            kv_other.astype(jnp.bfloat16),
-            q_regions,
-            k_regions,
-        )
-        final = finish_slot(embedded[s], mixed, w_out[...], o_gain_ref[...])
-        slot = lax.axis_index("buf") * slots + s
+    def _(k):
+        for h in range(2):
+            send(k, h).wait()
+            at = slice(half * h, half * (h + 1))
+            here = slice(windows // 2 * h, windows // 2 * (h + 1))
+            kv_other = jnp.dot(far[k, at], w_qkv[:, D:], preferred_element_type=jnp.float32)
+            mixed = attend_slot(
+                own_qkv[k, at, :D],
+                own_qkv[k, at, D:],
+                kv_other.astype(jnp.bfloat16),
+                q_regions[here],
+                k_regions[:, here],
+            )
+            finals[at] = finish_part(embedded[k, at], mixed, w_out[...], o_gain_ref[...])
+        final = from_windows(finals[...]).astype(jnp.bfloat16)
+        slot = lax.axis_index("buf") * slots + k
         taken = sample_ref[0] == slot
         for b in range(1, sample_ref.shape[0]):
             taken = jnp.logical_or(taken, sample_ref[b] == slot)
         final = jnp.where(taken, final, jnp.zeros_like(final))
-        flat = patches[s].reshape(rows_here * cols, patch_len)
-        patches[s] = decode_slot(flat, final, w_dec[...]).reshape(rows_here, cols, patch_len)
-        slot_out(s).start()
-
-    @pl.loop(0, slots)
-    def _(s):
-        slot_out(s).wait()
-
-
-def local_strips(store, sample_index, region_ids, w_embed, attn_gain, w_qkv, w_out, out_gain, w_dec):
+        flat = patches[k].reshape(tokens, patch_len)
+        new_ref[k] = decode_slot(flat, final, w_dec[...]).reshape(rows_here, cols, patch_len)
+
+
+def place_kernel(result_ref, new_ref, sems):
+    slots, rows = new_ref.shape[:2]
+    copies = [
+        pltpu.make_async_copy(result_ref.at[s, i], new_ref.at[s, i], sems.at[s, i])
+        for s in range(slots)
+        for i in range(rows)
+    ]
+    for copy in copies:
+        copy.start()
+    for copy in copies:
+        copy.wait()
+
+
+def local_strips(
+    store, sample_index, region_ids, w_embed, attn_gain, w_qkv, w_out, out_gain, w_dec
+):
     slots, rows_here, cols, patch_len = store.shape
     tokens = rows_here * cols
     held = lambda *shape: pltpu.VMEM(shape, jnp.bfloat16)
     vmem = pl.BlockSpec(memory_space=pltpu.VMEM)
     hbm = pl.BlockSpec(memory_space=pl.ANY)
-    return pl.pallas_call(
+    result = pl.pallas_call(
         fused_kernel,
         in_specs=[pl.BlockSpec(memory_space=pltpu.SMEM), vmem, vmem, vmem] + [hbm] * 5,
-        out_specs=hbm,
-        out_shape=jax.ShapeDtypeStruct(store.shape, store.dtype),
+        out_specs=vmem,
+        out_shape=pltpu.VMEM(store.shape, store.dtype),
         scratch_shapes=[
             held(*store.shape),
             held(*w_embed.shape),
@@ -364,11 +385,11 @@
             held(slots, tokens, D),
             held(slots, tokens, D),
             held(slots, tokens, 3 * D),
+            pltpu.VMEM((tokens, D), jnp.float32),
             pltpu.SemaphoreType.DMA((slots,)),
             pltpu.SemaphoreType.DMA((4,)),
-            pltpu.SemaphoreType.DMA((slots,)),
-            pltpu.SemaphoreType.DMA((slots,)),
-            pltpu.SemaphoreType.DMA((slots,)),
+            pltpu.SemaphoreType.DMA((slots, 2)),
+            pltpu.SemaphoreType.DMA((slots, 2)),
         ],
         compiler_params=pltpu.CompilerParams(
             vmem_limit_bytes=VMEM_LIMIT, collective_id=0, has_side_effects=True
@@ -384,6 +405,14 @@
         w_out,
         w_dec.T,
     )
+    return pl.pallas_call(
+        place_kernel,
+        in_specs=[hbm],
+        out_specs=hbm,
+        out_shape=jax.ShapeDtypeStruct(store.shape, store.dtype),
+        scratch_shapes=[pltpu.SemaphoreType.DMA((slots, rows_here))],
+        compiler_params=pltpu.CompilerParams(vmem_limit_bytes=PICK_LIMIT),
+    )(result)
 
 
 def local(store, *rest):

time: 37.5 us -> 34 us (0.907)
  local copies, waits for them, and re-layouts: 4.22 us -> 0 us
  Pallas kernels: 33.1 us -> 33.8 us
    unnamed x1 -> x0, local copies, waits for them, and re-layouts: 4.22 us -> none
    pallas_call x0 -> x1, Pallas kernels: none -> 1.96 us  [local_strips(): pl.pallas_call(place_kernel, in_specs=[hbm], out_specs=hbm, out_shape=jax...]
    pallas_call x1, Pallas kernels: 33.1 us -> 31.8 us  [local_strips(): pl.pallas_call(fused_kernel, in_specs=[pl.BlockSpec(memory_space=pltpu.SM...]
where the time goes in v3:
time: 34 us; the launch traced here: 33.8 us
  Pallas kernels  33.8 us (99%)
    pallas_call x1, Pallas kernels, local_strips(): pl.pallas_call(fused_kernel, in_specs=[pl.BlockSpec(memory_space=pltpu.SM...  31.8 us
    pallas_call x1, Pallas kernels, local_strips(): pl.pallas_call(place_kernel, in_specs=[hbm], out_specs=hbm, out_shape=jax...  1.96 us

profile of v3, /device:TPU:1, one launch (start us, length us, event | category | flops | bytes accessed | tf_op | source)
XLA Modules:
  0.0 33.8 jit_solution(819630507097990058)
XLA Ops:
  0.0 31.8 %shard_map.91.result_ref = bf16[4,4,64,1725]{3,2,1,0:T(8,128)(2,1)S(1)} custom-call(s32[6]{0:T(128)} %sample_ref.1, s32[64,64]{1,0:T(8,128)} %region_ref.1, f32[1,512]{1,0:T(1,128)} %bitcast.4, f32[1,512]{1,0:T(1,128)} %bitcast.5, bf16[4,4,64,1725]{3,2,1,0:T(8,128)(2,1)} %store_ref.1, bf16[1725,512]{1,0:T(8,128)(2,1)} %w_embed_ref.1, ...), custom_call_target="tpu_custom_call" | custom-call | tf_op jit(solution)/shard_map/pallas_call | solution.py:373
  31.8 2.0 %shard_map.92 = bf16[4,4,64,1725]{3,2,1,0:T(8,128)(2,1)} custom-call(bf16[4,4,64,1725]{3,2,1,0:T(8,128)(2,1)S(1)} %shard_map.91.result_ref), custom_call_target="tpu_custom_call" | custom-call | tf_op jit(solution)/shard_map/pallas_call | solution.py:408
